TPU v7x, 32 devices: a whole 2x2x4 slice. The times are simulated.
32 devices in a mesh: row: 4 (over y, x), col: 8 (over z, core).
Axes of the slice: x: 2, y: 2, z: 4, core: 2. Of those that a mesh axis runs over, the one named last changes fastest.
Arguments:
- tiles: bfloat16 [256, 256, 256], P(('row', 'col')), may hold values from -0.09375 to 0.09375
- tile_rows: int32 [256], P(('row', 'col')), may hold values from 0 to 3, as said below
- tile_cols: int32 [256], P(('row', 'col')), may hold values from 0 to 1
- tile_count: int32 [32], P(('row', 'col')), may hold values from 0 to 8, as said below
- bounds: float32 [2], replicated, may hold values from -1 to 2, as said below
- vectors: float32 [4096, 128], P(('row', 'col')), may hold values from -6 to 6
Outputs:
- filtered: float32 [4096, 128], P(('row', 'col'))
- gram: float32 [128, 128], replicated
Inputs may be any that keep to these rules, and one draw needn't show every extreme that they name: `tile_rows`: within each device the first tile_count slots name distinct blocks with global block row I <= global block column J; the device's diagonal blocks (I = J) come first; every diagonal block of the Hamiltonian is stored; slots after the live ones hold valid indices but are not part of the matrix. `tile_count`: devices whose block rows all lie below their block columns have no live slot; some device has all 8 slots live. bounds[0] < -0.5 and bounds[1] > 1.0.
All inputs are finite; a program needn't handle non-finite values.
Results may differ from a plain program's by a relative error of at most 0.0037.
Values may be sent and summed in bfloat16 or wider, within the bound.
A program may use at most 64 MiB of HBM per device.

v0:
```python
import jax
import jax.numpy as jnp
from jax import lax
from jax.sharding import PartitionSpec as P

BLK_COL = 2


def spread(block, axis, holder):
    block = jnp.where(lax.axis_index(axis) == holder, block, jnp.zeros_like(block))
    return lax.psum(block, axis)


def on_device(tiles, tile_rows, tile_cols, tile_count, bounds, vectors):
    col_ratio = lax.axis_size("col") // lax.axis_size("row")
    col_index = lax.axis_index("col")
    row_index = lax.axis_index("row")
    root_row = col_index // col_ratio
    slot_total = tiles.shape[0]
    block_size = tiles.shape[1]
    share_rows = vectors.shape[0]
    width_vecs = vectors.shape[1]
    group_rows = share_rows * lax.axis_size("col")
    group_blocks = group_rows // block_size
    column_rows = BLK_COL * block_size
    total_rows = share_rows * lax.axis_size("row") * lax.axis_size("col")
    offset = col_index % col_ratio * column_rows
    live_mask = (jnp.arange(slot_total, dtype=jnp.int32) < tile_count[0]).astype(jnp.bfloat16)
    owner_flag = (row_index == root_row).astype(jnp.float32)
    center = (bounds[1] + bounds[0]) * 0.5
    halfwidth = (bounds[1] - bounds[0]) * 0.5

    def apply_hamiltonian(current_vec):
        vector_panel = current_vec.astype(jnp.bfloat16)
        row_panel = lax.all_gather(vector_panel, "col", axis=0, tiled=True)
        col_piece = lax.dynamic_slice_in_dim(row_panel, offset, column_rows, 0)
        col_panel = spread(col_piece, "row", root_row)
        row_input = row_panel.reshape(group_blocks, block_size, width_vecs)
        col_input = col_panel.reshape(BLK_COL, block_size, width_vecs)
        start_rows = jnp.zeros((group_blocks, block_size, width_vecs), jnp.float32)
        start_cols = jnp.zeros((BLK_COL, block_size, width_vecs), jnp.float32)
        masked_cols = col_input[tile_cols] * live_mask[:, None, None]
        masked_rows = row_input[tile_rows] * live_mask[:, None, None]
        forward = jnp.einsum("tab,tbk->tak", tiles, masked_cols, preferred_element_type=jnp.float32)
        backward = jnp.einsum(
            "tab,tak->tbk", tiles, masked_rows, preferred_element_type=jnp.float32
        )
        row_part = start_rows.at[tile_rows].add(forward)
        col_part = start_cols.at[tile_cols].add(backward)
        column_total = lax.psum(col_part, "row")
        row_part = row_part.reshape(group_rows, width_vecs)
        present = lax.dynamic_slice_in_dim(row_part, offset, column_rows, 0)
        updated = present + owner_flag * column_total.reshape(column_rows, width_vecs)
        row_part = lax.dynamic_update_slice_in_dim(row_part, updated, offset, 0)
        return lax.psum_scatter(row_part, "col", scatter_dimension=0, tiled=True)

    current_vec = (apply_hamiltonian(vectors) - center * vectors) / halfwidth
    image = apply_hamiltonian(current_vec)
    following = 2.0 * (image - center * current_vec) / halfwidth - vectors
    current_vec = following
    gram_local = lax.dot_general(
        current_vec,
        current_vec,
        (((0,), (0,)), ((), ())),
        precision=lax.Precision.HIGHEST,
        preferred_element_type=jnp.float32,
    )
    gram_total = lax.psum(gram_local, ("row", "col"))
    return (current_vec, gram_total / total_rows)


def solution(mesh):
    in_specs = (
        P(("row", "col"), None, None),
        P(("row", "col")),
        P(("row", "col")),
        P(("row", "col")),
        P(),
        P(("row", "col"), None),
    )
    out_specs = (P(("row", "col"), None), P())
    return jax.shard_map(
        on_device, mesh=mesh, in_specs=in_specs, out_specs=out_specs, check_vma=False
    )
```

profile of v0, /device:TPU:1, one launch (start us, length us, event | category | flops | bytes accessed | tf_op | source)
XLA Modules:
  0.0 414.4 jit_solution(1064199134010569408)
XLA Ops:
  7.2 0.9 convert_element_type.16
  8.2 15.8 %all_gather.6 = bf16[1024,128]{1,0:T(8,128)(2,1)S(1)} all-gather(bf16[128,128]{1,0:T(8,128)(2,1)S(1)} %convert_element_type.16), channel_id=1, replica_groups=mesh['row'=4,'col'=8] {'col'}, dimensions={0}, use_global_device_ids=true | all-gather | bytes 294912 | tf_op jit(solution)/shard_map/all_gather | solution.py:35
  27.8 1.3 scatter_fusion.1
  29.9 37.0 %all-reduce.6.cloned.1.call-done = bf16[2,256,128]{2,1,0:T(8,128)(2,1)} async-done(((bf16[2,256,128]{2,1,0:T(8,128)(2,1)}), bf16[2,256,128]{2,1,0:T(8,128)(2,1)}) %all-reduce.6.cloned.1.call-update) | async-done | bytes 131088 | tf_op jit(solution)/shard_map/psum | solution.py:11
  66.9 1.5 gather_fusion
  68.5 1.7 convolution_bitcast_fusion.3
  70.2 1.5 copy.13
  71.8 1.3 scatter_fusion
  73.1 39.9 %all-reduce.8.cloned.1.call-done = f32[2,256,128]{2,1,0:T(8,128)} async-done(((f32[2,256,128]{2,1,0:T(8,128)}), f32[2,256,128]{2,1,0:T(8,128)}) %all-reduce.8.cloned.1.call-update) | async-done | bytes 262160 | tf_op jit(solution)/shard_map/psum | solution.py:50
  113.1 1.0 broadcast_multiply_fusion.1
  118.1 25.2 %reduce-scatter.3.cloned.1.call-done = f32[128,128]{1,0:T(8,128)} async-done(((f32[1024,128]{1,0:T(8,128)}), f32[128,128]{1,0:T(8,128)}) %reduce-scatter.3.cloned.1.call-update) | async-done | bytes 65552 | tf_op jit(solution)/shard_map/reduce_scatter | solution.py:55
  144.2 18.0 %all_gather.7 = bf16[1024,128]{1,0:T(8,128)(2,1)S(1)} all-gather(bf16[128,128]{1,0:T(8,128)(2,1)S(1)} %fusion.8), channel_id=1, replica_groups=mesh['row'=4,'col'=8] {'col'}, dimensions={0}, use_global_device_ids=true | all-gather | bytes 294912 | tf_op jit(solution)/shard_map/all_gather | solution.py:35
  164.4 1.3 scatter_fusion.3
  166.6 36.5 %all-reduce.10.cloned.1.call-done = bf16[2,256,128]{2,1,0:T(8,128)(2,1)} async-done(((bf16[2,256,128]{2,1,0:T(8,128)(2,1)}), bf16[2,256,128]{2,1,0:T(8,128)(2,1)}) %all-reduce.10.cloned.1.call-update) | async-done | bytes 131088 | tf_op jit(solution)/shard_map/psum | solution.py:11
  203.1 1.5 gather_fusion.2
  204.7 1.7 convolution_bitcast_fusion.1
  206.4 1.5 copy.17
  208.0 1.3 scatter_fusion.2
  209.3 39.5 %all-reduce.12.cloned.1.call-done = f32[2,256,128]{2,1,0:T(8,128)} async-done(((f32[2,256,128]{2,1,0:T(8,128)}), f32[2,256,128]{2,1,0:T(8,128)}) %all-reduce.12.cloned.1.call-update) | async-done | bytes 262160 | tf_op jit(solution)/shard_map/psum | solution.py:50
  248.8 1.0 broadcast_multiply_fusion
  250.7 28.2 %reduce-scatter.5.cloned.1.call-done = f32[128,128]{1,0:T(8,128)} async-done(((f32[1024,128]{1,0:T(8,128)}), f32[128,128]{1,0:T(8,128)}) %reduce-scatter.5.cloned.1.call-update) | async-done | bytes 65552 | tf_op jit(solution)/shard_map/reduce_scatter | solution.py:55
  279.8 0.9 fusion.10
  280.8 125.3 %all-reduce.14.cloned.1.call-done = f32[128,128]{1,0:T(8,128)} async-done(((f32[128,128]{1,0:T(8,128)}), f32[128,128]{1,0:T(8,128)}) %all-reduce.14.cloned.1.call-update) | async-done | bytes 65552 | tf_op jit(solution)/shard_map/psum | solution.py:68
  406.1 1.5 broadcast_multiply_fusion.2
  (58 shorter events, 11.0 us)
Async XLA Ops:
  7.2 19.5 %copy-start = (bf16[8,256,256]{2,1,0:T(8,128)(2,1)S(1)}, bf16[8,256,256]{2,1,0:T(8,128)(2,1)}, u32[]{:S(2)}) copy-start(bf16[8,256,256]{2,1,0:T(8,128)(2,1)} %param.6) | copy-start | bytes 3145732
  7.2 59.8 %all-reduce.6.cloned.1.call-start = ((), (), s32[]{:S(2)}) async-start(), calls=%async_computation.2 | async-start | bytes 262144 | tf_op jit(solution)/shard_map/psum | solution.py:11
  24.6 88.4 %all-reduce.8.cloned.1.call-start = ((), (), s32[]{:S(2)}) async-start(), calls=%async_computation.3 | async-start | bytes 524288 | tf_op jit(solution)/shard_map/psum | solution.py:50
  25.3 0.7 copy-start.9
  27.1 0.7 copy-start.10
  29.1 0.7 copy-start.4
  29.8 113.5 %reduce-scatter.3.cloned.1.call-start = ((), (), s32[]{:S(2)}) async-start(), calls=%async_computation.4 | async-start | bytes 589824 | tf_op jit(solution)/shard_map/reduce_scatter | solution.py:55
  114.1 0.8 copy-start.2
  114.1 0.9 copy-start.8
  114.1 29.3 %copy-start.5 = (f32[128,128]{1,0:T(8,128)S(1)}, f32[128,128]{1,0:T(8,128)}, u32[]{:S(2)}) copy-start(f32[128,128]{1,0:T(8,128)} %param.11) | copy-start | bytes 196612
  114.9 88.2 %all-reduce.10.cloned.1.call-start = ((), (), s32[]{:S(2)}) async-start(), calls=%async_computation.5 | async-start | bytes 262144 | tf_op jit(solution)/shard_map/psum | solution.py:11
  163.6 85.2 %all-reduce.12.cloned.1.call-start = ((), (), s32[]{:S(2)}) async-start(), calls=%async_computation.6 | async-start | bytes 524288 | tf_op jit(solution)/shard_map/psum | solution.py:50
  165.8 0.7 copy-start.3
  166.5 112.4 %reduce-scatter.5.cloned.1.call-start = ((), (), s32[]{:S(2)}) async-start(), calls=%async_computation.7 | async-start | bytes 589824 | tf_op jit(solution)/shard_map/reduce_scatter | solution.py:55
  249.9 0.8 copy-start.1
  249.9 29.1 %copy-start.7 = (f32[128,128]{1,0:T(8,128)S(1)}, f32[128,128]{1,0:T(8,128)}, u32[]{:S(2)}) copy-start(f32[128,128]{1,0:T(8,128)} %reduce-scatter.3.cloned.1.call-done) | copy-start | bytes 196612
  250.7 155.4 %all-reduce.14.cloned.1.call-start = ((), (), s32[]{:S(2)}) async-start(), calls=%async_computation.8 | async-start | bytes 131072 | tf_op jit(solution)/shard_map/psum | solution.py:68
  279.8 0.9 copy-start.6
Sparse Core Ops, SparseCore 0:
  24.8 42.1 all-reduce.5
  70.1 42.8 all-reduce.7
  115.3 28.0 reduce-scatter.2
  163.7 39.3 all-reduce.9
  205.9 42.9 all-reduce.11
  251.0 27.8 reduce-scatter.4
  285.1 120.9 all-reduce.13
where the time goes:
time: 415 us; the launch traced here: 414 us
  waiting for transfers between devices  332 us (80%)
  blocking collectives  33.8 us (8%)
  between operations  17.7 us (4%)
  local copies, waits for them, and re-layouts  12.8 us (3%)
  other arithmetic  12.8 us (3%)
  matrix products  5.15 us (1%)
    psum x1, waiting for transfers between devices, on_device(): gram_total = lax.psum(gram_local, ('row', 'col'))  125 us
    psum x2, waiting for transfers between devices, apply_hamiltonian(): column_total = lax.psum(col_part, 'row')  79.5 us
    psum x2, waiting for transfers between devices, spread(): return lax.psum(block, axis)  73.6 us
    reduce_scatter x2, waiting for transfers between devices, apply_hamiltonian(): return lax.psum_scatter(row_part, 'col', scatter_dimension=0, tiled=True)  53.5 us
    all_gather x2, blocking collectives, apply_hamiltonian(): row_panel = lax.all_gather(vector_panel, 'col', axis=0, tiled=True)  33.8 us
  transfers between devices with their start and end apart: 7, of which 7 were waited for; matrix products, arithmetic and copies ran while one was open for 4% of the time, Pallas kernels for 0%

commit v1 on v0

--- a/solution.py
+++ b/solution.py
@@ -32,7 +32,13 @@
 
     def apply_hamiltonian(current_vec):
         vector_panel = current_vec.astype(jnp.bfloat16)
-        row_panel = lax.all_gather(vector_panel, "col", axis=0, tiled=True)
+        count = lax.axis_size("col")
+        block_2, blocks = (vector_panel, [vector_panel])
+        for _ in range(count - 1):
+            block_2 = lax.ppermute(block_2, "col", [(i, (i + 1) % count) for i in range(count)])
+            blocks.insert(0, block_2)
+        line = jnp.concatenate(blocks, axis=0)
+        row_panel = jnp.roll(line, (lax.axis_index("col") + 1) * vector_panel.shape[0], axis=0)
         col_piece = lax.dynamic_slice_in_dim(row_panel, offset, column_rows, 0)
         col_panel = spread(col_piece, "row", root_row)
         row_input = row_panel.reshape(group_blocks, block_size, width_vecs)

time: 415 us -> 459 us (1.11)
  waiting for transfers between devices: 332 us -> 397 us
  blocking collectives: 33.8 us -> 0 us
  starting transfers between devices: 0.29 us -> 10 us
    ppermute x0 -> x14, waiting for transfers between devices: none -> 57.7 us  [apply_hamiltonian(): lax.ppermute(block_2, 'col', [(i, (i + 1) % count) for i in range(count)])]
    all_gather x2 -> x0, blocking collectives: 33.8 us -> none  [apply_hamiltonian(): row_panel = lax.all_gather(vector_panel, 'col', axis=0, tiled=True)]
    ppermute x0 -> x14, starting transfers between devices: none -> 9.71 us  [apply_hamiltonian(): lax.ppermute(block_2, 'col', [(i, (i + 1) % count) for i in range(count)])]
    psum x2, waiting for transfers between devices: 73.6 us -> 81.4 us  [spread(): return lax.psum(block, axis)]
  transfers between devices with their start and end apart: 7 -> 21, of which waited for: 7 -> 21; matrix products, arithmetic and copies ran while one was open for 4% -> 4% of each run, Pallas kernels for 0% -> 0%
where the time goes in v1:
time: 459 us
  waiting for transfers between devices  397 us (86%)
  between operations  17.7 us (4%)
  other arithmetic  15.6 us (3%)
  local copies, waits for them, and re-layouts  12.8 us (3%)
  starting transfers between devices  10 us (2%)
  matrix products  5.15 us (1%)
    psum x1, waiting for transfers between devices, on_device(): gram_total = lax.psum(gram_local, ('row', 'col'))  125 us
    psum x2, waiting for transfers between devices, spread(): return lax.psum(block, axis)  81.4 us
    psum x2, waiting for transfers between devices, apply_hamiltonian(): column_total = lax.psum(col_part, 'row')  79.5 us
    ppermute x14, waiting for transfers between devices, apply_hamiltonian(): lax.ppermute(block_2, 'col', [(i, (i + 1) % count) for i in range(count)])  57.7 us
    reduce_scatter x2, waiting for transfers between devices, apply_hamiltonian(): return lax.psum_scatter(row_part, 'col', scatter_dimension=0, tiled=True)  53.5 us
    ppermute x14, starting transfers between devices, apply_hamiltonian(): lax.ppermute(block_2, 'col', [(i, (i + 1) % count) for i in range(count)])  9.71 us
  transfers between devices with their start and end apart: 21, of which 21 were waited for; matrix products, arithmetic and copies ran while one was open for 4% of the time, Pallas kernels for 0%

profile of v1, /device:TPU:1, one launch (start us, length us, event | category | flops | bytes accessed | tf_op | source)
XLA Modules:
  0.0 458.7 jit_solution(7723361995786857978)
XLA Ops:
  8.2 2.7 collective-permute-start
  11.9 2.3 collective-permute-start.1
  15.2 2.3 collective-permute-start.2
  17.5 2.6 collective-permute-done.2
  20.9 4.4 collective-permute-done.3
  25.3 5.1 %collective-permute-done.4 = bf16[128,128]{1,0:T(8,128)(2,1)S(1)} collective-permute-done((bf16[128,128]{1,0:T(8,128)(2,1)S(1)}, bf16[128,128]{1,0:T(8,128)(2,1)S(1)}, u32[]{:S(2)}, u32[]{:S(2)}) %collective-permute-start.4) | collective-permute-done | bytes 32800 | tf_op jit(solution)/shard_map/ppermute | solution.py:38
  31.1 4.5 collective-permute-done.5
  35.6 5.1 %collective-permute-done.6 = bf16[128,128]{1,0:T(8,128)(2,1)S(1)} collective-permute-done((bf16[128,128]{1,0:T(8,128)(2,1)S(1)}, bf16[128,128]{1,0:T(8,128)(2,1)S(1)}, u32[]{:S(2)}, u32[]{:S(2)}) %collective-permute-start.6) | collective-permute-done | bytes 32800 | tf_op jit(solution)/shard_map/ppermute | solution.py:38
  47.3 40.6 %all-reduce.6.cloned.1.call-done = bf16[2,256,128]{2,1,0:T(8,128)(2,1)} async-done(((bf16[2,256,128]{2,1,0:T(8,128)(2,1)}), bf16[2,256,128]{2,1,0:T(8,128)(2,1)}) %all-reduce.6.cloned.1.call-update) | async-done | bytes 131088 | tf_op jit(solution)/shard_map/psum | solution.py:11
  89.5 1.7 convolution_bitcast_fusion.3
  94.1 39.9 %all-reduce.8.cloned.1.call-done = f32[2,256,128]{2,1,0:T(8,128)} async-done(((f32[2,256,128]{2,1,0:T(8,128)}), f32[2,256,128]{2,1,0:T(8,128)}) %all-reduce.8.cloned.1.call-update) | async-done | bytes 262160 | tf_op jit(solution)/shard_map/psum | solution.py:56
  139.1 25.2 %reduce-scatter.3.cloned.1.call-done = f32[128,128]{1,0:T(8,128)} async-done(((f32[1024,128]{1,0:T(8,128)}), f32[128,128]{1,0:T(8,128)}) %reduce-scatter.3.cloned.1.call-update) | async-done | bytes 65552 | tf_op jit(solution)/shard_map/reduce_scatter | solution.py:61
  166.8 3.2 collective-permute-done.7
  170.1 5.0 %collective-permute-done.8 = bf16[128,128]{1,0:T(8,128)(2,1)S(1)} collective-permute-done((bf16[128,128]{1,0:T(8,128)(2,1)S(1)}, bf16[128,128]{1,0:T(8,128)(2,1)S(1)}, u32[]{:S(2)}, u32[]{:S(2)}) %collective-permute-start.8) | collective-permute-done | bytes 32800 | tf_op jit(solution)/shard_map/ppermute | solution.py:38
  175.1 5.1 %collective-permute-done.9 = bf16[128,128]{1,0:T(8,128)(2,1)S(1)} collective-permute-done((bf16[128,128]{1,0:T(8,128)(2,1)S(1)}, bf16[128,128]{1,0:T(8,128)(2,1)S(1)}, u32[]{:S(2)}, u32[]{:S(2)}) %collective-permute-start.9) | collective-permute-done | bytes 32800 | tf_op jit(solution)/shard_map/ppermute | solution.py:38
  180.3 5.1 %collective-permute-done.10 = bf16[128,128]{1,0:T(8,128)(2,1)S(1)} collective-permute-done((bf16[128,128]{1,0:T(8,128)(2,1)S(1)}, bf16[128,128]{1,0:T(8,128)(2,1)S(1)}, u32[]{:S(2)}, u32[]{:S(2)}) %collective-permute-start.10) | collective-permute-done | bytes 32800 | tf_op jit(solution)/shard_map/ppermute | solution.py:38
  185.4 5.1 %collective-permute-done.11 = bf16[128,128]{1,0:T(8,128)(2,1)S(1)} collective-permute-done((bf16[128,128]{1,0:T(8,128)(2,1)S(1)}, bf16[128,128]{1,0:T(8,128)(2,1)S(1)}, u32[]{:S(2)}, u32[]{:S(2)}) %collective-permute-start.11) | collective-permute-done | bytes 32800 | tf_op jit(solution)/shard_map/ppermute | solution.py:38
  190.6 5.1 %collective-permute-done.12 = bf16[128,128]{1,0:T(8,128)(2,1)S(1)} collective-permute-done((bf16[128,128]{1,0:T(8,128)(2,1)S(1)}, bf16[128,128]{1,0:T(8,128)(2,1)S(1)}, u32[]{:S(2)}, u32[]{:S(2)}) %collective-permute-start.12) | collective-permute-done | bytes 32800 | tf_op jit(solution)/shard_map/ppermute | solution.py:38
  195.7 5.1 %collective-permute-done.13 = bf16[128,128]{1,0:T(8,128)(2,1)S(1)} collective-permute-done((bf16[128,128]{1,0:T(8,128)(2,1)S(1)}, bf16[128,128]{1,0:T(8,128)(2,1)S(1)}, u32[]{:S(2)}, u32[]{:S(2)}) %collective-permute-start.13) | collective-permute-done | bytes 32800 | tf_op jit(solution)/shard_map/ppermute | solution.py:38
  206.6 40.8 %all-reduce.10.cloned.1.call-done = bf16[2,256,128]{2,1,0:T(8,128)(2,1)} async-done(((bf16[2,256,128]{2,1,0:T(8,128)(2,1)}), bf16[2,256,128]{2,1,0:T(8,128)(2,1)}) %all-reduce.10.cloned.1.call-update) | async-done | bytes 131088 | tf_op jit(solution)/shard_map/psum | solution.py:11
  249.0 1.7 convolution_bitcast_fusion.1
  253.6 39.5 %all-reduce.12.cloned.1.call-done = f32[2,256,128]{2,1,0:T(8,128)} async-done(((f32[2,256,128]{2,1,0:T(8,128)}), f32[2,256,128]{2,1,0:T(8,128)}) %all-reduce.12.cloned.1.call-update) | async-done | bytes 262160 | tf_op jit(solution)/shard_map/psum | solution.py:56
  295.0 28.2 %reduce-scatter.5.cloned.1.call-done = f32[128,128]{1,0:T(8,128)} async-done(((f32[1024,128]{1,0:T(8,128)}), f32[128,128]{1,0:T(8,128)}) %reduce-scatter.5.cloned.1.call-update) | async-done | bytes 65552 | tf_op jit(solution)/shard_map/reduce_scatter | solution.py:61
  325.1 125.3 %all-reduce.14.cloned.1.call-done = f32[128,128]{1,0:T(8,128)} async-done(((f32[128,128]{1,0:T(8,128)}), f32[128,128]{1,0:T(8,128)}) %all-reduce.14.cloned.1.call-update) | async-done | bytes 65552 | tf_op jit(solution)/shard_map/psum | solution.py:74
  (102 shorter events, 35.0 us)
Async XLA Ops:
  7.2 37.3 %copy-start = (bf16[8,256,256]{2,1,0:T(8,128)(2,1)S(1)}, bf16[8,256,256]{2,1,0:T(8,128)(2,1)}, u32[]{:S(2)}) copy-start(bf16[8,256,256]{2,1,0:T(8,128)(2,1)} %param.8) | copy-start | bytes 3145732
  7.2 80.8 %all-reduce.6.cloned.1.call-start = ((), (), s32[]{:S(2)}) async-start(), calls=%async_computation.2 | async-start | bytes 262144 | tf_op jit(solution)/shard_map/psum | solution.py:11
  8.2 12.7 %copy-start.10 = (s32[8]{0:T(128)S(1)}, s32[8]{0:T(128)}, u32[]{:S(2)}) copy-start(s32[8]{0:T(128)} %param.10) | copy-start | bytes 100
  8.2 3.7 collective-permute-start
  11.9 3.3 collective-permute-start.1
  15.2 4.9 %collective-permute-start.2 = (bf16[128,128]{1,0:T(8,128)(2,1)S(1)}, bf16[128,128]{1,0:T(8,128)(2,1)S(1)}, u32[]{:S(2)}, u32[]{:S(2)}) collective-permute-start(bf16[128,128]{1,0:T(8,128)(2,1)S(1)} %collective-permute-done.1), channel_id=1, source_target_pairs={{0,1},{1,2},{2,3},{3,4},{4,5},{5,6},{6,7},{7,0},{8,9},{9,10},{10,1... | collective-permute-start | bytes 98312 | tf_op jit(solution)/shard_map/ppermute | solution.py:38
  20.1 5.1 %collective-permute-start.3 = (bf16[128,128]{1,0:T(8,128)(2,1)S(1)}, bf16[128,128]{1,0:T(8,128)(2,1)S(1)}, u32[]{:S(2)}, u32[]{:S(2)}) collective-permute-start(bf16[128,128]{1,0:T(8,128)(2,1)S(1)} %collective-permute-done.2), channel_id=1, source_target_pairs={{0,1},{1,2},{2,3},{3,4},{4,5},{5,6},{6,7},{7,0},{8,9},{9,10},{10,1... | collective-permute-start | bytes 98312 | tf_op jit(solution)/shard_map/ppermute | solution.py:38
  25.3 5.1 %collective-permute-start.4 = (bf16[128,128]{1,0:T(8,128)(2,1)S(1)}, bf16[128,128]{1,0:T(8,128)(2,1)S(1)}, u32[]{:S(2)}, u32[]{:S(2)}) collective-permute-start(bf16[128,128]{1,0:T(8,128)(2,1)S(1)} %collective-permute-done.3), channel_id=1, source_target_pairs={{0,1},{1,2},{2,3},{3,4},{4,5},{5,6},{6,7},{7,0},{8,9},{9,10},{10,1... | collective-permute-start | bytes 98312 | tf_op jit(solution)/shard_map/ppermute | solution.py:38
  30.4 5.1 %collective-permute-start.5 = (bf16[128,128]{1,0:T(8,128)(2,1)S(1)}, bf16[128,128]{1,0:T(8,128)(2,1)S(1)}, u32[]{:S(2)}, u32[]{:S(2)}) collective-permute-start(bf16[128,128]{1,0:T(8,128)(2,1)S(1)} %collective-permute-done.4), channel_id=1, source_target_pairs={{0,1},{1,2},{2,3},{3,4},{4,5},{5,6},{6,7},{7,0},{8,9},{9,10},{10,1... | collective-permute-start | bytes 98312 | tf_op jit(solution)/shard_map/ppermute | solution.py:38
  35.6 5.1 %collective-permute-start.6 = (bf16[128,128]{1,0:T(8,128)(2,1)S(1)}, bf16[128,128]{1,0:T(8,128)(2,1)S(1)}, u32[]{:S(2)}, u32[]{:S(2)}) collective-permute-start(bf16[128,128]{1,0:T(8,128)(2,1)S(1)} %collective-permute-done.5), channel_id=1, source_target_pairs={{0,1},{1,2},{2,3},{3,4},{4,5},{5,6},{6,7},{7,0},{8,9},{9,10},{10,1... | collective-permute-start | bytes 98312 | tf_op jit(solution)/shard_map/ppermute | solution.py:38
  43.7 90.3 %all-reduce.8.cloned.1.call-start = ((), (), s32[]{:S(2)}) async-start(), calls=%async_computation.3 | async-start | bytes 524288 | tf_op jit(solution)/shard_map/psum | solution.py:56
  47.3 117.1 %reduce-scatter.3.cloned.1.call-start = ((), (), s32[]{:S(2)}) async-start(), calls=%async_computation.4 | async-start | bytes 589824 | tf_op jit(solution)/shard_map/reduce_scatter | solution.py:61
  135.9 111.5 %all-reduce.10.cloned.1.call-start = ((), (), s32[]{:S(2)}) async-start(), calls=%async_computation.5 | async-start | bytes 262144 | tf_op jit(solution)/shard_map/psum | solution.py:11
  165.2 4.8 %collective-permute-start.7 = (bf16[128,128]{1,0:T(8,128)(2,1)S(1)}, bf16[128,128]{1,0:T(8,128)(2,1)S(1)}, u32[]{:S(2)}, u32[]{:S(2)}) collective-permute-start(bf16[128,128]{1,0:T(8,128)(2,1)S(1)} %fusion.14), channel_id=1, source_target_pairs={{0,1},{1,2},{2,3},{3,4},{4,5},{5,6},{6,7},{7,0},{8,9},{9,10},{10,1... | collective-permute-start | bytes 98312 | tf_op jit(solution)/shard_map/ppermute | solution.py:38
  170.0 5.1 %collective-permute-start.8 = (bf16[128,128]{1,0:T(8,128)(2,1)S(1)}, bf16[128,128]{1,0:T(8,128)(2,1)S(1)}, u32[]{:S(2)}, u32[]{:S(2)}) collective-permute-start(bf16[128,128]{1,0:T(8,128)(2,1)S(1)} %collective-permute-done.7), channel_id=1, source_target_pairs={{0,1},{1,2},{2,3},{3,4},{4,5},{5,6},{6,7},{7,0},{8,9},{9,10},{10,1... | collective-permute-start | bytes 98312 | tf_op jit(solution)/shard_map/ppermute | solution.py:38
  175.1 5.1 %collective-permute-start.9 = (bf16[128,128]{1,0:T(8,128)(2,1)S(1)}, bf16[128,128]{1,0:T(8,128)(2,1)S(1)}, u32[]{:S(2)}, u32[]{:S(2)}) collective-permute-start(bf16[128,128]{1,0:T(8,128)(2,1)S(1)} %collective-permute-done.8), channel_id=1, source_target_pairs={{0,1},{1,2},{2,3},{3,4},{4,5},{5,6},{6,7},{7,0},{8,9},{9,10},{10,1... | collective-permute-start | bytes 98312 | tf_op jit(solution)/shard_map/ppermute | solution.py:38
  180.3 5.1 %collective-permute-start.10 = (bf16[128,128]{1,0:T(8,128)(2,1)S(1)}, bf16[128,128]{1,0:T(8,128)(2,1)S(1)}, u32[]{:S(2)}, u32[]{:S(2)}) collective-permute-start(bf16[128,128]{1,0:T(8,128)(2,1)S(1)} %collective-permute-done.9), channel_id=1, source_target_pairs={{0,1},{1,2},{2,3},{3,4},{4,5},{5,6},{6,7},{7,0},{8,9},{9,10},{10,1... | collective-permute-start | bytes 98312 | tf_op jit(solution)/shard_map/ppermute | solution.py:38
  185.4 5.1 %collective-permute-start.11 = (bf16[128,128]{1,0:T(8,128)(2,1)S(1)}, bf16[128,128]{1,0:T(8,128)(2,1)S(1)}, u32[]{:S(2)}, u32[]{:S(2)}) collective-permute-start(bf16[128,128]{1,0:T(8,128)(2,1)S(1)} %collective-permute-done.10), channel_id=1, source_target_pairs={{0,1},{1,2},{2,3},{3,4},{4,5},{5,6},{6,7},{7,0},{8,9},{9,10},{10,1... | collective-permute-start | bytes 98312 | tf_op jit(solution)/shard_map/ppermute | solution.py:38
  190.6 5.1 %collective-permute-start.12 = (bf16[128,128]{1,0:T(8,128)(2,1)S(1)}, bf16[128,128]{1,0:T(8,128)(2,1)S(1)}, u32[]{:S(2)}, u32[]{:S(2)}) collective-permute-start(bf16[128,128]{1,0:T(8,128)(2,1)S(1)} %collective-permute-done.11), channel_id=1, source_target_pairs={{0,1},{1,2},{2,3},{3,4},{4,5},{5,6},{6,7},{7,0},{8,9},{9,10},{10,1... | collective-permute-start | bytes 98312 | tf_op jit(solution)/shard_map/ppermute | solution.py:38
  195.7 5.1 %collective-permute-start.13 = (bf16[128,128]{1,0:T(8,128)(2,1)S(1)}, bf16[128,128]{1,0:T(8,128)(2,1)S(1)}, u32[]{:S(2)}, u32[]{:S(2)}) collective-permute-start(bf16[128,128]{1,0:T(8,128)(2,1)S(1)} %collective-permute-done.12), channel_id=1, source_target_pairs={{0,1},{1,2},{2,3},{3,4},{4,5},{5,6},{6,7},{7,0},{8,9},{9,10},{10,1... | collective-permute-start | bytes 98312 | tf_op jit(solution)/shard_map/ppermute | solution.py:38
  203.7 89.4 %all-reduce.12.cloned.1.call-start = ((), (), s32[]{:S(2)}) async-start(), calls=%async_computation.6 | async-start | bytes 524288 | tf_op jit(solution)/shard_map/psum | solution.py:56
  206.6 116.6 %reduce-scatter.5.cloned.1.call-start = ((), (), s32[]{:S(2)}) async-start(), calls=%async_computation.7 | async-start | bytes 589824 | tf_op jit(solution)/shard_map/reduce_scatter | solution.py:61
  294.2 29.1 %copy-start.7 = (f32[128,128]{1,0:T(8,128)S(1)}, f32[128,128]{1,0:T(8,128)}, u32[]{:S(2)}) copy-start(f32[128,128]{1,0:T(8,128)} %reduce-scatter.3.cloned.1.call-done) | copy-start | bytes 196612
  295.0 155.4 %all-reduce.14.cloned.1.call-start = ((), (), s32[]{:S(2)}) async-start(), calls=%async_computation.8 | async-start | bytes 131072 | tf_op jit(solution)/shard_map/psum | solution.py:74
  (8 other events, 16.0 us)
Sparse Core Ops, SparseCore 0:
  43.8 44.0 all-reduce.5
  91.1 42.8 all-reduce.7
  136.3 28.0 reduce-scatter.2
  203.8 43.5 all-reduce.9
  250.2 42.9 all-reduce.11
  295.3 27.8 reduce-scatter.4
  329.4 120.9 all-reduce.13
